TPU v7x, 32 devices: a whole 2x2x4 slice. The times are simulated.
32 devices in a mesh: dom: 8 (over z, core), sub: 4 (over y, x).
Axes of the slice: x: 2, y: 2, z: 4, core: 2. Of those that a mesh axis runs over, the one named last changes fastest.
Arguments:
- state: float32 [9, 10, 8192], P(None, None, ('dom', 'sub')), may hold values from -6 to 6
- geometry: float32 [3, 3, 8192], P(None, None, ('dom', 'sub')), may hold values from -4 to 4
- face_scale: float32 [4, 8192], P(None, ('dom', 'sub')), may hold values from 0.2 to 1
- material: int32 [8192], P(('dom', 'sub')), may hold values from 0 to 2
- cluster: int32 [8192], P(('dom', 'sub')), may hold values from 0 to 1, as said below
- neighbours: int32 [4, 8192], P(None, ('dom', 'sub')), may hold values from 0 to 767, as said below
- orientation: int32 [4, 8192], P(None, ('dom', 'sub')), may hold values from 0 to 11
- stiffness: float32 [3, 10, 10], replicated, may hold values from -2 to 2
- jacobians: float32 [3, 3, 9, 9], replicated, may hold values from -2 to 2
- flux_local: float32 [4, 10, 10], replicated, may hold values from -2 to 2
- flux_neigh: float32 [12, 10, 10], replicated, may hold values from -2 to 2
- flux_plus: float32 [3, 9, 9], replicated, may hold values from -2 to 2
- flux_minus: float32 [3, 9, 9], replicated, may hold values from -2 to 2
Outputs:
- final_state: float32 [9, 10, 8192], P(None, None, ('dom', 'sub'))
Inputs may be any that keep to these rules, and one draw needn't show every extreme that they name: Face neighbours are numbered in the table of the face's own partition, as the first step says. `cluster`: 0 marks a fine tetrahedron, 1 a coarse one.
All inputs are finite; a program needn't handle non-finite values.
Results may differ from a plain program's by a relative error of at most 0.0003.
Values sent between devices are 32-bit elements; how exact they have to be, the bound alone decides.
A program may use at most 64 MiB of HBM per device.

v0:
```python
import jax
import jax.numpy as jnp
from jax import lax
from jax.sharding import PartitionSpec as P

COPY_DEV = 128
SUB_COPY = 64


step_length = 0.2


def from_behind(block, axis, distance):
    devices = range(lax.axis_size(axis))
    route = [((i - distance) % len(devices), i) for i in devices]
    return lax.ppermute(block, axis, route)


def per_element(matrix, values):
    total = matrix[:, 0][:, None, :] * values[0][None, :, :]
    for inner in range(1, matrix.shape[1]):
        total = total + matrix[:, inner][:, None, :] * values[inner][None, :, :]
    return total


def per_element_basis(matrix, values):
    total = matrix[None, :, 0, :] * values[:, 0][:, None, :]
    for inner in range(1, matrix.shape[1]):
        total = total + matrix[None, :, inner, :] * values[:, inner][:, None, :]
    return total


def apply_star(values, stiffness, geometry, element_jac, transpose):
    pattern = "ba,vbe->vae" if transpose else "ab,vbe->vae"
    mapped = [
        jnp.einsum(pattern, stiffness[direction], values, precision=lax.Precision.HIGHEST)
        for direction in range(3)
    ]
    summed = jnp.zeros_like(values)
    for column in range(3):
        mixture = (
            mapped[0] * geometry[0, column]
            + mapped[1] * geometry[1, column]
            + mapped[2] * geometry[2, column]
        )
        summed = summed + per_element(element_jac[column], mixture)
    return summed


def predict(values, stiffness, geometry, element_jac, coarse, shifted):
    first = -apply_star(values, stiffness, geometry, element_jac, False)
    second = -apply_star(first, stiffness, geometry, element_jac, False)
    if shifted:
        values = values + coarse * (step_length * first + 0.5 * step_length**2 * second)
        first = first + coarse * (step_length * second)
    return step_length * values + step_length**2 / 2 * first + step_length**3 / 6 * second


def update(
    own,
    neighbour_parts,
    face_scale,
    stiffness,
    geometry,
    element_jac,
    element_plus,
    element_minus,
    face_neigh,
    flux_local,
):
    result = apply_star(own, stiffness, geometry, element_jac, True)
    plus = per_element(element_plus, own)
    for face in range(4):
        minus = per_element(element_minus, neighbour_parts[face])
        across = jnp.einsum("ab,vbe->vae", flux_local[face], plus, precision=lax.Precision.HIGHEST)
        across = across + per_element_basis(face_neigh[face], minus)
        result = result - face_scale[face] * across
    return result


def element_tables(material, orientation, jacobians, flux_plus, flux_minus, flux_neigh):
    medium_mask = (material[None, :] == jnp.arange(3, dtype=jnp.int32)[:, None]).astype(jnp.float32)
    element_jac = jnp.einsum(
        "mcvw,me->cvwe", jacobians, medium_mask, precision=lax.Precision.HIGHEST
    )
    element_plus = jnp.einsum(
        "mvw,me->vwe", flux_plus, medium_mask, precision=lax.Precision.HIGHEST
    )
    element_minus = jnp.einsum(
        "mvw,me->vwe", flux_minus, medium_mask, precision=lax.Precision.HIGHEST
    )
    turns = jnp.arange(12, dtype=jnp.int32)[:, None]
    face_neigh = [
        jnp.einsum(
            "tab,te->abe",
            flux_neigh,
            (orientation[face][None, :] == turns).astype(jnp.float32),
            precision=lax.Precision.HIGHEST,
        )
        for face in range(4)
    ]
    return (element_jac, element_plus, element_minus, face_neigh)


def share(lower, upper):
    from_group = lax.all_gather(lower[:, :, :SUB_COPY], "sub", axis=2, tiled=True)
    from_left = from_behind(upper, "dom", 1)
    from_right = from_behind(lower, "dom", -1)
    return [from_group, from_left, from_right]


def shards(
    state,
    geometry,
    face_scale,
    material,
    cluster,
    neighbours,
    orientation,
    stiffness,
    jacobians,
    flux_local,
    flux_neigh,
    flux_plus,
    flux_minus,
):
    count = state.shape[2]
    element_jac, element_plus, element_minus, face_neigh = element_tables(
        material, orientation, jacobians, flux_plus, flux_minus, flux_neigh
    )
    coarse = cluster.astype(jnp.float32)
    finer = 1.0 - coarse

    def integrate(values, shifted):
        whole = predict(values, stiffness, geometry, element_jac, coarse, shifted)
        outside = share(whole[:, :, :COPY_DEV], whole[:, :, count - COPY_DEV :])
        return (whole, jnp.concatenate([whole] + outside, axis=2))

    def advance(values, shifted):
        integral, table = integrate(values, shifted)
        parts = [jnp.take(table, neighbours[face], axis=2) for face in range(4)]
        return update(
            integral,
            parts,
            face_scale,
            stiffness,
            geometry,
            element_jac,
            element_plus,
            element_minus,
            face_neigh,
            flux_local,
        )

    first_change = advance(state, False)
    middle = state + finer * first_change
    second_change = advance(middle, True)
    state = middle + finer * second_change + coarse * (first_change + second_change)
    return state


def solution(mesh):
    placed = (
        P(None, None, ("dom", "sub")),
        P(None, None, ("dom", "sub")),
        P(None, ("dom", "sub")),
        P(("dom", "sub")),
        P(("dom", "sub")),
        P(None, ("dom", "sub")),
        P(None, ("dom", "sub")),
        P(),
        P(),
        P(),
        P(),
        P(),
        P(),
    )
    return jax.shard_map(
        shards, mesh=mesh, in_specs=placed, out_specs=P(None, None, ("dom", "sub")), check_vma=False
    )
```

profile of v0, /device:TPU:0, one launch (start us, length us, event | category | flops | bytes accessed | tf_op | source)
XLA Modules:
  0.0 184.3 jit_solution(13740262639894165088)
XLA Ops:
  4.2 1.3 convolution_bitcast_fusion
  9.5 4.5 %collective-permute-start.1 = (f32[9,10,128]{2,1,0:T(8,128)}, f32[9,10,128]{2,1,0:T(8,128)}, u32[]{:S(2)}, u32[]{:S(2)}) collective-permute-start(f32[9,10,128]{2,1,0:T(8,128)} %get-tuple-element.348), channel_id=1, source_target_pairs={{4,0},{8,4},{12,8},{16,12},{20,16},{24,20},{28,24},{0,28},{5,1},{9... | collective-permute-start | bytes 138248 | tf_op jit(solution)/shard_map/ppermute | solution.py:16
  39.9 20.4 %all_gather.6 = f32[9,10,256]{1,0,2:T(8,128)S(1)} all-gather(f32[9,10,64]{1,0,2:T(8,128)S(1)} %copy.139), channel_id=1, replica_groups=mesh['dom'=8,'sub'=4] {'sub'}, dimensions={2}, use_global_device_ids=true | all-gather | bytes 115200 | tf_op jit(solution)/shard_map/all_gather | solution.py:106
  62.0 5.0 %copy.141 = f32[9,10,768]{1,0,2:T(8,128)} copy(f32[9,10,768]{2,1,0:T(8,128)S(1)} %pad_maximum_fusion) | data formatting | bytes 552960 | tf_op jit(solution)/shard_map/concatenate | solution.py:137
  67.0 3.7 %gather_fusion.3 = f32[256,9,10]{2,1,0:T(8,128)S(1)} fusion(f32[9,10,768]{1,0,2:T(8,128)} %copy.141, s32[1024]{0:T(1024)} %pad_clamp_fusion), kind=kCustom, calls=%fused_computation.3.clone | custom fusion | bytes 185344 | tf_op jit(solution)/shard_map/jit(_take)/gather | solution.py:141
  73.4 3.7 %gather_fusion.2 = f32[256,9,10]{2,1,0:T(8,128)S(1)} fusion(f32[9,10,768]{1,0,2:T(8,128)} %copy.141, s32[1024]{0:T(1024)} %pad_clamp_fusion.1), kind=kCustom, calls=%fused_computation.2.clone | custom fusion | bytes 185344 | tf_op jit(solution)/shard_map/jit(_take)/gather | solution.py:141
  79.8 3.7 %gather_fusion.1 = f32[256,9,10]{2,1,0:T(8,128)S(1)} fusion(f32[9,10,768]{1,0,2:T(8,128)} %copy.141, s32[1024]{0:T(1024)} %pad_clamp_fusion.2), kind=kCustom, calls=%fused_computation.1.clone | custom fusion | bytes 185344 | tf_op jit(solution)/shard_map/jit(_take)/gather | solution.py:141
  86.2 3.5 %gather_fusion = f32[256,9,10]{2,1,0:T(8,128)S(1)} fusion(f32[9,10,768]{1,0,2:T(8,128)} %copy.141, s32[1024]{0:T(1024)S(1)} %pad_clamp_fusion.3), kind=kCustom, calls=%fused_computation.clone | custom fusion | bytes 185344 | tf_op jit(solution)/shard_map/jit(_take)/gather | solution.py:141
  96.3 2.5 %multiply_add_fusion.11 = (f32[9,10,256]{2,1,0:T(8,128)S(1)}, f32[9,10,256]{2,1,0:T(8,128)}) fusion(f32[9,10,256]{2,1,0:T(8,128)S(1)} %copy-done.2, f32[256]{0:T(256)} %get-tuple-element.477, f32[9,10,256]{2,1,0:T(8,128)S(1)} %fusion.15, f32[9,10,256]{2,1,0:T(8,128)S(1)} %fusion.14, f32[9,10,256]{2,1,0:T(8,128)S(1)} %fusion.13, ...), kind=kOutput, calls=%fused_computation.81 | convolution fusion | flops 4608000 | bytes 1367440 | tf_op jit(solution)/shard_map/ab,vbe->vae/dot_general | solution.py:75
  104.1 3.0 %collective-permute-start.3 = (f32[9,10,128]{2,1,0:T(8,128)}, f32[9,10,128]{2,1,0:T(8,128)S(1)}, u32[]{:S(2)}, u32[]{:S(2)}) collective-permute-start(f32[9,10,128]{2,1,0:T(8,128)} %get-tuple-element.247), channel_id=1, source_target_pairs={{4,0},{8,4},{12,8},{16,12},{20,16},{24,20},{28,24},{0,28},{5,1},{9... | collective-permute-start | bytes 138248 | tf_op jit(solution)/shard_map/ppermute | solution.py:16
  110.6 22.0 %all_gather.7 = f32[9,10,256]{1,0,2:T(8,128)S(1)} all-gather(f32[9,10,64]{1,0,2:T(8,128)S(1)} %copy.190), channel_id=1, replica_groups=mesh['dom'=8,'sub'=4] {'sub'}, dimensions={2}, use_global_device_ids=true | all-gather | bytes 115200 | tf_op jit(solution)/shard_map/all_gather | solution.py:106
  133.4 5.0 %copy.192 = f32[9,10,768]{1,0,2:T(8,128)} copy(f32[9,10,768]{2,1,0:T(8,128)S(1)} %pad_maximum_fusion.1) | data formatting | bytes 552960 | tf_op jit(solution)/shard_map/concatenate | solution.py:137
  138.4 5.0 %gather_fusion.7 = f32[256,9,10]{2,1,0:T(8,128)} fusion(f32[9,10,768]{1,0,2:T(8,128)} %copy.192, s32[1024]{0:T(1024)} %pad_clamp_fusion), kind=kCustom, calls=%fused_computation.7.clone | custom fusion | bytes 185344 | tf_op jit(solution)/shard_map/jit(_take)/gather | solution.py:141
  143.4 5.0 %gather_fusion.6 = f32[256,9,10]{2,1,0:T(8,128)} fusion(f32[9,10,768]{1,0,2:T(8,128)} %copy.192, s32[1024]{0:T(1024)} %pad_clamp_fusion.1), kind=kCustom, calls=%fused_computation.6.clone | custom fusion | bytes 185344 | tf_op jit(solution)/shard_map/jit(_take)/gather | solution.py:141
  148.4 5.0 %gather_fusion.5 = f32[256,9,10]{2,1,0:T(8,128)} fusion(f32[9,10,768]{1,0,2:T(8,128)} %copy.192, s32[1024]{0:T(1024)} %pad_clamp_fusion.2), kind=kCustom, calls=%fused_computation.5.clone | custom fusion | bytes 185344 | tf_op jit(solution)/shard_map/jit(_take)/gather | solution.py:141
  153.4 3.7 %gather_fusion.4 = f32[256,9,10]{2,1,0:T(8,128)S(1)} fusion(f32[9,10,768]{1,0,2:T(8,128)} %copy.192, s32[1024]{0:T(1024)} %copy-done.149), kind=kCustom, calls=%fused_computation.4.clone | custom fusion | bytes 185344 | tf_op jit(solution)/shard_map/jit(_take)/gather | solution.py:141
  157.1 1.9 %select_bitcast_fusion = f32[9,10,256]{1,0,2:T(8,128)S(1)} fusion(f32[256,9,10]{2,1,0:T(8,128)} %gather_fusion.7, pred[256]{0:T(512)(128)(4,1)S(1)} %copy-done.160), kind=kLoop, calls=%fused_computation.8 | loop fusion | flops 23040 | bytes 184576 | tf_op jit(solution)/shard_map/jit(_take)/select_n | solution.py:141
  159.0 1.3 fusion.66
  162.8 1.9 %select_bitcast_fusion.1 = f32[9,10,256]{1,0,2:T(8,128)S(1)} fusion(f32[256,9,10]{2,1,0:T(8,128)} %gather_fusion.6, pred[256]{0:T(512)(128)(4,1)} %compare_and_fusion.1), kind=kLoop, calls=%fused_computation.9 | loop fusion | flops 23040 | bytes 184576 | tf_op jit(solution)/shard_map/jit(_take)/select_n | solution.py:141
  164.8 1.3 fusion.65
  168.6 1.9 %select_bitcast_fusion.2 = f32[9,10,256]{1,0,2:T(8,128)S(1)} fusion(f32[256,9,10]{2,1,0:T(8,128)} %gather_fusion.5, pred[256]{0:T(512)(128)(4,1)} %compare_and_fusion.2), kind=kLoop, calls=%fused_computation.10 | loop fusion | flops 23040 | bytes 184576 | tf_op jit(solution)/shard_map/jit(_take)/select_n | solution.py:141
  170.5 1.3 fusion.64
  178.7 1.3 fusion.22
  181.6 2.6 %multiply_add_fusion.8 = f32[9,10,256]{2,1,0:T(8,128)} fusion(f32[9,10,256]{2,1,0:T(8,128)} %get-tuple-element.479, f32[9,10,256]{2,1,0:T(8,128)S(1)} %get-tuple-element.478, f32[9,10,256]{2,1,0:T(8,128)S(1)} %fusion.23, f32[9,10,256]{2,1,0:T(8,128)S(1)} %fusion.22, f32[9,10,256]{2,1,0:T(8,128)S(1)} %fusion.21, f32[9,10,256]{2,1,0:T(8,128)S(1)} %copy-done.68, ...), kind=kOutput, calls=%fused_computation.68 | convolution fusion | flops 4677120 | bytes 1368464 | tf_op jit(solution)/shard_map/ab,vbe->vae/dot_general | solution.py:75
  (572 shorter events, 70.2 us)
Async XLA Ops:
  5.7 95.5 %copy-start.3 = (f32[9,1,256]{2,0,1:T(8,128)}, f32[9,1,256]{2,0,1:T(8,128)S(1)}, u32[]{:S(2)}) copy-start(f32[9,1,256]{2,0,1:T(8,128)S(1)} %copy.482) | copy-start | bytes 27652
  5.8 95.5 %copy-start.5 = (f32[9,1,256]{2,0,1:T(8,128)}, f32[9,1,256]{2,0,1:T(8,128)S(1)}, u32[]{:S(2)}) copy-start(f32[9,1,256]{2,0,1:T(8,128)S(1)} %copy.483) | copy-start | bytes 27652
  5.8 95.5 %copy-start.7 = (f32[9,1,256]{2,0,1:T(8,128)}, f32[9,1,256]{2,0,1:T(8,128)S(1)}, u32[]{:S(2)}) copy-start(f32[9,1,256]{2,0,1:T(8,128)S(1)} %copy.484) | copy-start | bytes 27652
  5.8 95.5 %copy-start.9 = (f32[9,1,256]{2,0,1:T(8,128)}, f32[9,1,256]{2,0,1:T(8,128)S(1)}, u32[]{:S(2)}) copy-start(f32[9,1,256]{2,0,1:T(8,128)S(1)} %copy.485) | copy-start | bytes 27652
  5.8 95.5 %copy-start.11 = (f32[9,1,256]{2,0,1:T(8,128)}, f32[9,1,256]{2,0,1:T(8,128)S(1)}, u32[]{:S(2)}) copy-start(f32[9,1,256]{2,0,1:T(8,128)S(1)} %copy.486) | copy-start | bytes 27652
  6.2 95.1 %copy-start.13 = (f32[9,1,256]{2,0,1:T(8,128)}, f32[9,1,256]{2,0,1:T(8,128)S(1)}, u32[]{:S(2)}) copy-start(f32[9,1,256]{2,0,1:T(8,128)S(1)} %copy.487) | copy-start | bytes 27652
  6.2 95.1 %copy-start.15 = (f32[9,1,256]{2,0,1:T(8,128)}, f32[9,1,256]{2,0,1:T(8,128)S(1)}, u32[]{:S(2)}) copy-start(f32[9,1,256]{2,0,1:T(8,128)S(1)} %copy.488) | copy-start | bytes 27652
  6.2 95.1 %copy-start.17 = (f32[9,1,256]{2,0,1:T(8,128)}, f32[9,1,256]{2,0,1:T(8,128)S(1)}, u32[]{:S(2)}) copy-start(f32[9,1,256]{2,0,1:T(8,128)S(1)} %copy.489) | copy-start | bytes 27652
  6.3 95.1 %copy-start.19 = (f32[9,1,256]{2,0,1:T(8,128)}, f32[9,1,256]{2,0,1:T(8,128)S(1)}, u32[]{:S(2)}) copy-start(f32[9,1,256]{2,0,1:T(8,128)S(1)} %copy.490) | copy-start | bytes 27652
  6.3 95.1 %copy-start.21 = (f32[9,1,256]{2,0,1:T(8,128)}, f32[9,1,256]{2,0,1:T(8,128)S(1)}, u32[]{:S(2)}) copy-start(f32[9,1,256]{2,0,1:T(8,128)S(1)} %copy.491) | copy-start | bytes 27652
  6.3 95.1 %copy-start.23 = (f32[9,1,256]{2,0,1:T(8,128)}, f32[9,1,256]{2,0,1:T(8,128)S(1)}, u32[]{:S(2)}) copy-start(f32[9,1,256]{2,0,1:T(8,128)S(1)} %copy.492) | copy-start | bytes 27652
  6.3 95.1 %copy-start.25 = (f32[9,1,256]{2,0,1:T(8,128)}, f32[9,1,256]{2,0,1:T(8,128)S(1)}, u32[]{:S(2)}) copy-start(f32[9,1,256]{2,0,1:T(8,128)S(1)} %copy.493) | copy-start | bytes 27652
  6.4 95.0 %copy-start.27 = (f32[9,1,256]{2,0,1:T(8,128)}, f32[9,1,256]{2,0,1:T(8,128)S(1)}, u32[]{:S(2)}) copy-start(f32[9,1,256]{2,0,1:T(8,128)S(1)} %copy.494) | copy-start | bytes 27652
  6.4 95.0 %copy-start.29 = (f32[9,1,256]{2,0,1:T(8,128)}, f32[9,1,256]{2,0,1:T(8,128)S(1)}, u32[]{:S(2)}) copy-start(f32[9,1,256]{2,0,1:T(8,128)S(1)} %copy.495) | copy-start | bytes 27652
  6.4 95.0 %copy-start.31 = (f32[9,256]{1,0:T(8,128)}, f32[9,256]{1,0:T(8,128)S(1)}, u32[]{:S(2)}) copy-start(f32[9,256]{1,0:T(8,128)S(1)} %get-tuple-element.498) | copy-start | bytes 27652
  6.4 95.0 %copy-start.33 = (f32[9,256]{1,0:T(8,128)}, f32[9,256]{1,0:T(8,128)S(1)}, u32[]{:S(2)}) copy-start(f32[9,256]{1,0:T(8,128)S(1)} %get-tuple-element.499) | copy-start | bytes 27652
  6.5 95.0 %copy-start.35 = (f32[9,256]{1,0:T(8,128)}, f32[9,256]{1,0:T(8,128)S(1)}, u32[]{:S(2)}) copy-start(f32[9,256]{1,0:T(8,128)S(1)} %get-tuple-element.500) | copy-start | bytes 27652
  6.5 95.0 %copy-start.37 = (f32[9,256]{1,0:T(8,128)}, f32[9,256]{1,0:T(8,128)S(1)}, u32[]{:S(2)}) copy-start(f32[9,256]{1,0:T(8,128)S(1)} %get-tuple-element.501) | copy-start | bytes 27652
  6.5 89.5 %copy-start.41 = (f32[9,256]{1,0:T(8,128)}, f32[9,256]{1,0:T(8,128)S(1)}, u32[]{:S(2)}) copy-start(f32[9,256]{1,0:T(8,128)S(1)} %get-tuple-element.503) | copy-start | bytes 27652
  6.5 94.9 %copy-start.39 = (f32[9,256]{1,0:T(8,128)}, f32[9,256]{1,0:T(8,128)S(1)}, u32[]{:S(2)}) copy-start(f32[9,256]{1,0:T(8,128)S(1)} %get-tuple-element.502) | copy-start | bytes 27652
  9.5 51.5 %collective-permute-start.1 = (f32[9,10,128]{2,1,0:T(8,128)}, f32[9,10,128]{2,1,0:T(8,128)}, u32[]{:S(2)}, u32[]{:S(2)}) collective-permute-start(f32[9,10,128]{2,1,0:T(8,128)} %get-tuple-element.348), channel_id=1, source_target_pairs={{4,0},{8,4},{12,8},{16,12},{20,16},{24,20},{28,24},{0,28},{5,1},{9... | collective-permute-start | bytes 138248 | tf_op jit(solution)/shard_map/ppermute | solution.py:16
  14.0 47.0 %collective-permute-start = (f32[9,10,128]{2,1,0:T(8,128)}, f32[9,10,128]{2,1,0:T(8,128)}, u32[]{:S(2)}, u32[]{:S(2)}) collective-permute-start(f32[9,10,128]{2,1,0:T(8,128)} %get-tuple-element.347), channel_id=1, source_target_pairs={{28,0},{0,4},{4,8},{8,12},{12,16},{16,20},{20,24},{24,28},{29,1},{... | collective-permute-start | bytes 138248 | tf_op jit(solution)/shard_map/ppermute | solution.py:16
  104.1 29.2 %collective-permute-start.3 = (f32[9,10,128]{2,1,0:T(8,128)}, f32[9,10,128]{2,1,0:T(8,128)S(1)}, u32[]{:S(2)}, u32[]{:S(2)}) collective-permute-start(f32[9,10,128]{2,1,0:T(8,128)} %get-tuple-element.247), channel_id=1, source_target_pairs={{4,0},{8,4},{12,8},{16,12},{20,16},{24,20},{28,24},{0,28},{5,1},{9... | collective-permute-start | bytes 138248 | tf_op jit(solution)/shard_map/ppermute | solution.py:16
  107.1 26.2 %collective-permute-start.2 = (f32[9,10,128]{2,1,0:T(8,128)}, f32[9,10,128]{2,1,0:T(8,128)S(1)}, u32[]{:S(2)}, u32[]{:S(2)}) collective-permute-start(f32[9,10,128]{2,1,0:T(8,128)} %get-tuple-element.246), channel_id=1, source_target_pairs={{28,0},{0,4},{4,8},{8,12},{12,16},{16,20},{20,24},{24,28},{29,1},{... | collective-permute-start | bytes 138248 | tf_op jit(solution)/shard_map/ppermute | solution.py:16
  (141 other events, 1200.4 us)
where the time goes:
time: 186 us; the launch traced here: 184 us
  local copies, waits for them, and re-layouts  88.7 us (48%)
  blocking collectives  42.4 us (23%)
  matrix products  22.5 us (12%)
  other arithmetic  19.7 us (11%)
  starting transfers between devices  7.46 us (4%)
  between operations  3.53 us (2%)
    all_gather x2, blocking collectives, share(): lax.all_gather(lower[:, :, :SUB_COPY], 'sub', axis=2, tiled=True)  42.4 us
    gather x8, local copies, waits for them, and re-layouts, advance(): parts = [jnp.take(table, neighbours[face], axis=2) for face in range(4)]  33.2 us
    unnamed x375, local copies, waits for them, and re-layouts  13 us
    dot_general x8, matrix products, update(): jnp.einsum('ab,vbe->vae', flux_local[face], plus, precision=lax.Precision...  12.4 us
    concatenate x2, local copies, waits for them, and re-layouts, integrate(): return (whole, jnp.concatenate([whole] + outside, axis=2))  10.1 us
    slice x12, local copies, waits for them, and re-layouts, per_element(): total = matrix[:, 0][:, None, :] * values[0][None, :, :]  8.7 us
    mul x64, local copies, waits for them, and re-layouts, per_element(): total = total + matrix[:, inner][:, None, :] * values[inner][None, :, :]  8.24 us
    select_n x12, other arithmetic, advance(): parts = [jnp.take(table, neighbours[face], axis=2) for face in range(4)]  8.16 us
  transfers between devices with their start and end apart: 4, of which 0 were waited for; matrix products, arithmetic and copies ran while one was open for 16% of the time, Pallas kernels for 0%

commit v1 on v0

v1 whole, which is shorter than its diff:
```python
import functools

import jax
import jax.numpy as jnp
from jax import lax
from jax.experimental import pallas as pl
from jax.experimental.pallas import tpu as pltpu
from jax.sharding import PartitionSpec as P

COPY_DEV = 128
SUB_COPY = 64
QUANT = 9
BASIS = 10
GROUP = 32
ROWS = 96
BLOCKS = 5
WIDE = 512

step_length = 0.2
f32 = jnp.float32
bf16 = jnp.bfloat16
MESH = pl.DeviceIdType.MESH


def iota(shape, dim):
    return lax.broadcasted_iota(jnp.int32, shape, dim)


def place(row):
    inner = row & (GROUP - 1)
    third = (inner >= BASIS).astype(jnp.int32) + (inner >= 2 * BASIS).astype(jnp.int32)
    quantity = 3 * lax.shift_right_logical(row, 5) + third
    return quantity, third, inner - BASIS * third, inner < 3 * BASIS


def split(values):
    high = values.astype(bf16)
    return high, (values - high.astype(f32)).astype(bf16)


def mul(a, b):
    return jnp.dot(a, b, preferred_element_type=f32)


def row_of(quantity):
    return GROUP * (quantity // 3) + BASIS * (quantity % 3)


def kernel(
    n_dom,
    n_sub,
    state_ref,
    geometry_ref,
    scale_ref,
    material_ref,
    cluster_ref,
    neighbours_ref,
    orientation_ref,
    stiffness_ref,
    jacobians_ref,
    local_ref,
    neigh_ref,
    plus_ref,
    minus_ref,
    out_ref,
    dofs,
    small,
    tiled,
    basis,
    fluxes,
    wide_high,
    wide_low,
    right_high,
    right_low,
    hot,
    table,
    picked_high,
    picked_low,
    ends,
    packed,
    from_sub,
    from_dom,
    send_sem,
    recv_sem,
):
    count = state_ref.shape[2]
    dom, sub = lax.axis_index("dom"), lax.axis_index("sub")
    left = (lax.rem(dom + n_dom - 1, n_dom), sub)
    right = (lax.rem(dom + 1, n_dom), sub)
    peers = [(dom, lax.rem(sub + k, n_sub)) for k in range(1, n_sub)]

    barrier = pltpu.get_barrier_semaphore()
    for other in [left, right] + peers:
        pl.semaphore_signal(barrier, inc=1, device_id=other, device_id_type=MESH)

    small[...] = jnp.zeros_like(small)
    for i in range(3):
        small[i, :BASIS, :BASIS] = stiffness_ref[i]
    for i in range(4):
        small[6 + i, :BASIS, :BASIS] = local_ref[i]
    for i in range(12):
        small[10 + i, :BASIS, :BASIS] = neigh_ref[i]
    col = iota((16, ROWS), 1)
    _, _, fn, ok = place(col)
    hit = (iota((16, ROWS), 0) == fn) & ok
    pick_high = jnp.where(hit & (col < 2 * GROUP), 1.0, 0.0).astype(bf16)
    pick_low = jnp.where(hit & (col >= 2 * GROUP), 1.0, 0.0).astype(bf16)
    for i in range(3):
        small[3 + i, :, :16] = small[i][:, :16].T
    high, low = split(small[...].reshape(22 * 16, 128)[:, :16])
    spread = (mul(high, pick_high) + mul(low, pick_low)).reshape(22, 16, ROWS)
    tiled[...] = jnp.zeros_like(tiled)
    for third in range(3):
        tiled[:, BASIS * third : BASIS * third + BASIS, :] = spread[:, :BASIS, :]
    shape = (22, GROUP, ROWS)
    _, third_row, _, ok_row = place(iota(shape, 1))
    _, third_col, _, ok_col = place(iota(shape, 2) & (GROUP - 1))
    keep = (third_row == third_col) & ok_row & ok_col
    basis[...] = jnp.where(keep, tiled[...], 0.0).astype(bf16).reshape(22 * GROUP, ROWS)

    fluxes[...] = jnp.zeros_like(fluxes)
    for m in range(3):
        for c in range(3):
            fluxes[c, m, :QUANT, :QUANT] = jacobians_ref[m, c]
        fluxes[3, m, :QUANT, :QUANT] = -plus_ref[m]
        fluxes[4, m, :QUANT, :QUANT] = -minus_ref[m]
    high, low = split(fluxes[...].reshape(BLOCKS * 48, 128)[:, :16])
    rows_high, rows_low = 0.0, 0.0
    for k in range(BLOCKS):
        col = iota((16, WIDE), 1) - ROWS * k
        quantity, _, _, ok = place(col & 127)
        hit = (col >= 0) & (col < ROWS) & ok & (quantity == iota((16, WIDE), 0))
        pick = jnp.where(hit, 1.0, 0.0).astype(bf16)
        rows_high = rows_high + mul(high[48 * k : 48 * k + 48], pick)
        rows_low = rows_low + mul(low[48 * k : 48 * k + 48], pick)
    quantity, _, fn_row, ok_row = place(iota((ROWS, WIDE), 0))
    _, _, fn_col, ok_col = place(iota((ROWS, WIDE), 1))
    keep = (fn_row == fn_col) & ok_row & ok_col & (iota((ROWS, WIDE), 1) < BLOCKS * ROWS)
    quantity, _, _, ok = place(iota((ROWS, 16), 0))
    pick = jnp.where((quantity == iota((ROWS, 16), 1)) & ok, 1.0, 0.0).astype(bf16)
    rows_high, rows_low = rows_high.astype(bf16), rows_low.astype(bf16)
    for m in range(3):
        whole = mul(pick, rows_high[16 * m : 16 * m + 16])
        wide_high[ROWS * m : ROWS * m + ROWS, :] = jnp.where(keep, whole, 0.0).astype(bf16)
        whole = mul(pick, rows_low[16 * m : 16 * m + 16])
        wide_low[ROWS * m : ROWS * m + ROWS, :] = jnp.where(keep, whole, 0.0).astype(bf16)

    pad = jnp.zeros((WIDE - BLOCKS * ROWS, count), bf16)
    right_high[BLOCKS * ROWS :, :] = pad
    right_low[BLOCKS * ROWS :, :] = pad

    dofs[...] = jnp.zeros_like(dofs)
    for v in range(QUANT):
        dofs[row_of(v) : row_of(v) + BASIS, :] = state_ref[v]

    material = jnp.broadcast_to(material_ref[...], (ROWS, count))
    coarse = jnp.broadcast_to(cluster_ref[...], (ROWS, count)).astype(f32)

    def on_basis(high, low, first, last):
        parts = []
        for g in range(3):
            h, l = high[GROUP * g : GROUP * g + GROUP], low[GROUP * g : GROUP * g + GROUP]
            parts.append(mul(basis[GROUP * first : GROUP * last, :], jnp.concatenate([h, l, h], axis=0)))
        return [
            jnp.concatenate([part[GROUP * k : GROUP * k + GROUP] for part in parts], axis=0)
            for k in range(last - first)
        ]

    def mixtures(mapped):
        for c in range(3):
            mixture = (
                mapped[0] * geometry_ref[0, c : c + 1, :]
                + mapped[1] * geometry_ref[1, c : c + 1, :]
                + mapped[2] * geometry_ref[2, c : c + 1, :]
            )
            h, l = split(mixture)
            right_high[ROWS * c : ROWS * c + ROWS, :] = h
            right_low[ROWS * c : ROWS * c + ROWS, :] = l

    def on_quantities(depth):
        every = (
            mul(wide_high[:, :depth], right_high[:depth, :])
            + mul(wide_high[:, :depth], right_low[:depth, :])
            + mul(wide_low[:, :depth], right_high[:depth, :])
        )
        return jnp.where(
            material == 0,
            every[:ROWS],
            jnp.where(material == 1, every[ROWS : 2 * ROWS], every[2 * ROWS :]),
        )

    def star(values):
        high, low = split(values)
        mixtures(on_basis(high, low, 0, 3))
        return on_quantities(3 * ROWS)

    def predict(values, shifted):
        first = -star(values)
        second = -star(first)
        if shifted:
            values = values + coarse * (step_length * first + 0.5 * step_length**2 * second)
            first = first + coarse * (step_length * second)
        return step_length * values + step_length**2 / 2 * first + step_length**3 / 6 * second

    def halves(values, lanes):
        high, low = split(values)
        table[:ROWS, lanes] = high
        table[ROWS:, lanes] = low

    lane = iota((ROWS // 2, COPY_DEV), 1)
    front = lane < SUB_COPY

    def send(integral, r):
        ends[r, 0] = integral[:, :COPY_DEV]
        ends[r, 1] = integral[:, count - COPY_DEV :]
        top, bottom = integral[: ROWS // 2, :COPY_DEV], integral[ROWS // 2 :, :COPY_DEV]
        mine = jnp.where(front, top, pltpu.roll(bottom, SUB_COPY, 1))
        packed[r] = mine
        from_sub[r, sub] = mine
        if r == 0:
            pl.semaphore_wait(barrier, n_sub + 1)
        copies = []
        for k, (end, other) in enumerate([(1, right), (0, left)]):
            copies.append(
                pltpu.make_async_remote_copy(
                    src_ref=ends.at[r, end],
                    dst_ref=from_dom.at[r, k],
                    send_sem=send_sem.at[r, k],
                    recv_sem=recv_sem.at[r, k],
                    device_id=other,
                    device_id_type=MESH,
                )
            )
        for k, other in enumerate(peers):
            copies.append(
                pltpu.make_async_remote_copy(
                    src_ref=packed.at[r],
                    dst_ref=from_sub.at[r, sub],
                    send_sem=send_sem.at[r, 2 + k],
                    recv_sem=recv_sem.at[r, 2 + k],
                    device_id=other,
                    device_id_type=MESH,
                )
            )
        for copy in copies:
            copy.start()
        return copies

    depth = hot.shape[0]

    def advance(values, r):
        integral = predict(values, r == 1)
        copies = send(integral, r)
        if r == 0:
            for f in range(4):
                wanted = jnp.broadcast_to(neighbours_ref[f : f + 1, :], (depth, count))
                hit = jnp.where(iota((depth, count), 0) == wanted, 1.0, 0.0)
                hot[:, count * f : count * f + count] = hit.astype(bf16)
        high, low = split(integral)
        table[:ROWS, :count] = high
        table[ROWS:, :count] = low
        mapped = on_basis(high, low, 3, 10)
        mixtures(mapped[:3])
        local = mapped[3] * scale_ref[0:1, :]
        for f in range(1, 4):
            local = local + mapped[3 + f] * scale_ref[f : f + 1, :]
        h, l = split(local)
        right_high[3 * ROWS : 4 * ROWS, :] = h
        right_low[3 * ROWS : 4 * ROWS, :] = l

        for copy in copies:
            copy.wait()
        for pair in range(n_sub // 2):
            one, two = from_sub[r, 2 * pair], from_sub[r, 2 * pair + 1]
            top = jnp.where(front, one, pltpu.roll(two, SUB_COPY, 1))
            bottom = jnp.where(front, pltpu.roll(one, SUB_COPY, 1), two)
            lanes = slice(count + 128 * pair, count + 128 * pair + 128)
            halves(jnp.concatenate([top, bottom], axis=0), lanes)
        for k in range(2):
            start = count + SUB_COPY * n_sub + COPY_DEV * k
            halves(from_dom[r, k], slice(start, start + COPY_DEV))

        for f in range(4):
            lanes = slice(count * f, count * f + count)
            found = mul(table[...], hot[:, lanes])
            picked_high[:, lanes] = found[:ROWS].astype(bf16)
            picked_low[:, lanes] = found[ROWS:].astype(bf16)
        for g in range(3):
            rows = slice(GROUP * g, GROUP * g + GROUP)
            total = 0.0
            for f in range(4):
                lanes = slice(count * f, count * f + count)
                h, l = picked_high[rows, lanes], picked_low[rows, lanes]
                turned = mul(basis[10 * GROUP :, :], jnp.concatenate([h, l, h], axis=0))
                turn = jnp.broadcast_to(orientation_ref[f : f + 1, :], (GROUP, count))
                chosen = turned[:GROUP]
                for t in range(1, 12):
                    chosen = jnp.where(turn == t, turned[GROUP * t : GROUP * t + GROUP], chosen)
                total = total + chosen * scale_ref[f : f + 1, :]
            h, l = split(total)
            right_high[4 * ROWS + GROUP * g : 4 * ROWS + GROUP * g + GROUP, :] = h
            right_low[4 * ROWS + GROUP * g : 4 * ROWS + GROUP * g + GROUP, :] = l
        return on_quantities(WIDE)

    state = dofs[...]
    first_change = advance(state, 0)
    middle = state + (1.0 - coarse) * first_change
    second_change = advance(middle, 1)
    dofs[...] = middle + second_change + coarse * first_change
    for v in range(QUANT):
        out_ref[v] = dofs[row_of(v) : row_of(v) + BASIS, :]


def shards(n_dom, n_sub, state, geometry, face_scale, material, cluster, *rest):
    count = state.shape[2]
    depth = count + SUB_COPY * n_sub + 2 * COPY_DEV
    vmem = pl.BlockSpec(memory_space=pltpu.VMEM)
    copies = n_sub + 1
    return pl.pallas_call(
        functools.partial(kernel, n_dom, n_sub),
        out_shape=jax.ShapeDtypeStruct(state.shape, f32),
        in_specs=[vmem] * 13,
        out_specs=vmem,
        scratch_shapes=[
            pltpu.VMEM((ROWS, count), f32),
            pltpu.VMEM((22, 16, 128), f32),
            pltpu.VMEM((22, GROUP, ROWS), f32),
            pltpu.VMEM((22 * GROUP, ROWS), bf16),
            pltpu.VMEM((BLOCKS, 3, 16, 128), f32),
            pltpu.VMEM((3 * ROWS, WIDE), bf16),
            pltpu.VMEM((3 * ROWS, WIDE), bf16),
            pltpu.VMEM((WIDE, count), bf16),
            pltpu.VMEM((WIDE, count), bf16),
            pltpu.VMEM((depth, 4 * count), bf16),
            pltpu.VMEM((2 * ROWS, depth), bf16),
            pltpu.VMEM((ROWS, 4 * count), bf16),
            pltpu.VMEM((ROWS, 4 * count), bf16),
            pltpu.VMEM((2, 2, ROWS, COPY_DEV), f32),
            pltpu.VMEM((2, ROWS // 2, COPY_DEV), f32),
            pltpu.VMEM((2, n_sub, ROWS // 2, COPY_DEV), f32),
            pltpu.VMEM((2, 2, ROWS, COPY_DEV), f32),
            pltpu.SemaphoreType.DMA((2, copies)),
            pltpu.SemaphoreType.DMA((2, copies)),
        ],
        compiler_params=pltpu.CompilerParams(
            collective_id=0, has_side_effects=True, vmem_limit_bytes=48 * 1024 * 1024
        ),
    )(state, geometry, face_scale, material[None], cluster[None], *rest)


def solution(mesh):
    placed = (
        P(None, None, ("dom", "sub")),
        P(None, None, ("dom", "sub")),
        P(None, ("dom", "sub")),
        P(("dom", "sub")),
        P(("dom", "sub")),
        P(None, ("dom", "sub")),
        P(None, ("dom", "sub")),
        P(),
        P(),
        P(),
        P(),
        P(),
        P(),
    )
    return jax.shard_map(
        functools.partial(shards, mesh.shape["dom"], mesh.shape["sub"]),
        mesh=mesh,
        in_specs=placed,
        out_specs=P(None, None, ("dom", "sub")),
        check_vma=False,
    )
```

time: 186 us -> 22.6 us (0.12)
  local copies, waits for them, and re-layouts: 88.7 us -> 3.82 us
  blocking collectives: 42.4 us -> 0 us
  matrix products: 22.5 us -> 0 us
  other arithmetic: 19.7 us -> 0 us
  Pallas kernels: 0 us -> 18.4 us
  starting transfers between devices: 7.46 us -> 0 us
  between operations: 3.53 us -> 0.09 us
    all_gather x2 -> x0, blocking collectives: 42.4 us -> none  [share(): lax.all_gather(lower[:, :, :SUB_COPY], 'sub', axis=2, tiled=True)]
    gather x8 -> x0, local copies, waits for them, and re-layouts: 33.2 us -> none  [advance(): parts = [jnp.take(table, neighbours[face], axis=2) for face in range(4)]]
    dot_general x33 -> x0, matrix products: 22.5 us -> none  [the longest x8 12.4 us: update(): jnp.einsum('ab,vbe->vae', flux_local[face], plus, precision=lax.Precision...]
    pallas_call x0 -> x1, Pallas kernels: none -> 18.4 us  [shards(): pl.pallas_call(functools.partial(kernel, n_dom, n_sub), out_shape=jax.Sha...]
    mul x99 -> x0, local copies, waits for them, and re-layouts: 17.2 us -> none  [the longest x64 8.24 us: per_element(): total = total + matrix[:, inner][:, None, :] * values[inner][None, :, :]]
    slice x28 -> x0, local copies, waits for them, and re-layouts: 13.9 us -> none  [the longest x12 8.7 us: per_element(): total = matrix[:, 0][:, None, :] * values[0][None, :, :]]
    concatenate x2 -> x0, local copies, waits for them, and re-layouts: 10.1 us -> none  [integrate(): return (whole, jnp.concatenate([whole] + outside, axis=2))]
    unnamed x375 -> x31, local copies, waits for them, and re-layouts: 13 us -> 3.82 us
  transfers between devices with their start and end apart: 4 -> 0, of which waited for: 0 -> 0; matrix products, arithmetic and copies ran while one was open for 16% -> 0% of each run, Pallas kernels for 0% -> 0%
where the time goes in v1:
time: 22.6 us; the launch traced here: 22.3 us
  Pallas kernels  18.4 us (81%)
  local copies, waits for them, and re-layouts  3.82 us (17%)
    pallas_call x1, Pallas kernels, shards(): pl.pallas_call(functools.partial(kernel, n_dom, n_sub), out_shape=jax.Sha...  18.4 us
    unnamed x31, local copies, waits for them, and re-layouts  3.82 us

profile of v1, /device:TPU:0, one launch (start us, length us, event | category | flops | bytes accessed | tf_op | source)
XLA Modules:
  0.0 22.3 jit_solution(14673817950357003387)
XLA Ops:
  0.0 0.0 copy-start.10
  0.0 0.7 %copy.14.stiffness_ref = f32[3,10,10]{2,1,0:T(8,128)S(1)} copy(f32[3,10,10]{2,0,1:T(4,128)} %param.20) | data formatting | bytes 2400 | tf_op args[7]
  0.7 0.0 copy-done.10
  0.7 0.0 copy-start.11
  0.7 0.0 copy-start.9
  0.8 0.7 %copy-done.11 = f32[3,9,9]{2,0,1:T(4,128)S(1)} copy-done((f32[3,9,9]{2,0,1:T(4,128)S(1)}, f32[3,9,9]{2,0,1:T(4,128)}, u32[]{:S(2)}) %copy-start.11) | copy-done | bytes 996
  1.5 0.0 copy-start.8
  1.5 0.0 copy-done.9
  1.5 0.0 copy-start.7
  1.5 0.8 %copy-done.8 = f32[3,3,9,9]{3,1,2,0:T(4,128)S(1)} copy-done((f32[3,3,9,9]{3,1,2,0:T(4,128)S(1)}, f32[3,3,9,9]{3,1,2,0:T(4,128)}, u32[]{:S(2)}) %copy-start.8) | copy-done | bytes 2940
  2.3 0.0 copy-start
  2.3 0.1 copy-done.7
  2.4 0.0 copy-start.1
  2.4 0.0 copy-start.5
  2.4 0.0 copy-start.6
  2.5 0.7 %copy-done = f32[9,10,256]{2,1,0:T(8,128)S(1)} copy-done((f32[9,10,256]{2,1,0:T(8,128)S(1)}, f32[9,10,256]{2,1,0:T(8,128)}, u32[]{:S(2)}) %copy-start) | copy-done | bytes 92184
  3.2 0.0 copy-done.1
  3.2 0.0 copy-done.2
  3.2 0.0 copy-done.3
  3.2 0.0 copy-done.4
  3.2 0.0 copy-done.5
  3.2 0.0 copy-done.6
  3.2 18.4 %shard_map.127 = f32[9,10,256]{2,1,0:T(8,128)S(1)} custom-call(f32[9,10,256]{2,1,0:T(8,128)S(1)} %copy-done, f32[3,3,256]{2,1,0:T(4,128)S(1)} %copy-done.1, f32[4,256]{1,0:T(4,128)S(1)} %copy-done.2, s32[1,256]{1,0:T(1,128)S(1)} %bitcast.2, s32[1,256]{1,0:T(1,128)S(1)} %bitcast.3, s32[4,256]{1,0:T(4,128)S(1)} %copy-done.3, s32[4,256]{1,0:T(4,128)S(1)} %copy-done.4, ...), custom_call_target="tpu_custom_call" | custom-call | tf_op jit(solution)/shard_map/pallas_call | solution.py:319
  21.6 0.7 %copy.21 = f32[9,10,256]{2,1,0:T(8,128)} copy(f32[9,10,256]{2,1,0:T(8,128)S(1)} %shard_map.127) | data formatting | bytes 184320
  (8 shorter events, 0.0 us)
Async XLA Ops:
  0.0 0.7 %copy-start.10 = (f32[3,9,9]{2,0,1:T(4,128)S(1)}, f32[3,9,9]{2,0,1:T(4,128)}, u32[]{:S(2)}) copy-start(f32[3,9,9]{2,0,1:T(4,128)} %param.24) | copy-start | bytes 2920
  0.7 0.7 %copy-start.11 = (f32[3,9,9]{2,0,1:T(4,128)S(1)}, f32[3,9,9]{2,0,1:T(4,128)}, u32[]{:S(2)}) copy-start(f32[3,9,9]{2,0,1:T(4,128)} %param.25) | copy-start | bytes 2920
  0.7 0.7 %copy-start.9 = (f32[4,10,10]{2,0,1:T(4,128)S(1)}, f32[4,10,10]{2,0,1:T(4,128)}, u32[]{:S(2)}) copy-start(f32[4,10,10]{2,0,1:T(4,128)} %param.22) | copy-start | bytes 4804
  1.5 0.8 %copy-start.8 = (f32[3,3,9,9]{3,1,2,0:T(4,128)S(1)}, f32[3,3,9,9]{3,1,2,0:T(4,128)}, u32[]{:S(2)}) copy-start(f32[3,3,9,9]{3,1,2,0:T(4,128)} %param.21) | copy-start | bytes 8752
  1.5 0.9 %copy-start.7 = (f32[12,10,10]{2,0,1:T(8,128)S(1)}, f32[12,10,10]{2,0,1:T(8,128)}, u32[]{:S(2)}) copy-start(f32[12,10,10]{2,0,1:T(8,128)} %param.23) | copy-start | bytes 14404
  2.3 0.9 %copy-start = (f32[9,10,256]{2,1,0:T(8,128)S(1)}, f32[9,10,256]{2,1,0:T(8,128)}, u32[]{:S(2)}) copy-start(f32[9,10,256]{2,1,0:T(8,128)} %state_ref.1) | copy-start | bytes 276484
  2.4 0.8 %copy-start.1 = (f32[3,3,256]{2,1,0:T(4,128)S(1)}, f32[3,3,256]{2,1,0:T(4,128)}, u32[]{:S(2)}) copy-start(f32[3,3,256]{2,1,0:T(4,128)} %geometry_ref.1) | copy-start | bytes 27652
  2.4 0.8 %copy-start.2 = (f32[4,256]{1,0:T(4,128)S(1)}, f32[4,256]{1,0:T(4,128)}, u32[]{:S(2)}) copy-start(f32[4,256]{1,0:T(4,128)} %scale_ref.1) | copy-start | bytes 12292
  2.4 0.8 %copy-start.3 = (s32[4,256]{1,0:T(4,128)S(1)}, s32[4,256]{1,0:T(4,128)}, u32[]{:S(2)}) copy-start(s32[4,256]{1,0:T(4,128)} %neighbours_ref.1) | copy-start | bytes 12292
  2.4 0.8 %copy-start.4 = (s32[4,256]{1,0:T(4,128)S(1)}, s32[4,256]{1,0:T(4,128)}, u32[]{:S(2)}) copy-start(s32[4,256]{1,0:T(4,128)} %orientation_ref.1) | copy-start | bytes 12292
  2.4 0.8 %copy-start.5 = (s32[256]{0:T(256)S(1)}, s32[256]{0:T(256)}, u32[]{:S(2)}) copy-start(s32[256]{0:T(256)} %param.16) | copy-start | bytes 3076
  2.4 0.8 %copy-start.6 = (s32[256]{0:T(256)S(1)}, s32[256]{0:T(256)}, u32[]{:S(2)}) copy-start(s32[256]{0:T(256)} %param.17) | copy-start | bytes 3076

commit v2 on v1

v2 whole, which is shorter than its diff:
```python
import functools

import jax
import jax.numpy as jnp
from jax import lax
from jax.experimental import pallas as pl
from jax.experimental.pallas import tpu as pltpu
from jax.sharding import PartitionSpec as P

COPY_DEV = 128
SUB_COPY = 64
QUANT = 9
BASIS = 10
GROUP = 32
ROWS = 96
SLOTS = 24
LIMIT = 62 * 1024 * 1024

step_length = 0.2
f32 = jnp.float32
bf16 = jnp.bfloat16
MESH = pl.DeviceIdType.MESH


def iota(shape, dim):
    return lax.broadcasted_iota(jnp.int32, shape, dim)


def place(row):
    inner = row & (GROUP - 1)
    third = (inner >= BASIS).astype(jnp.int32) + (inner >= 2 * BASIS).astype(jnp.int32)
    quantity = 3 * lax.shift_right_logical(row, 5) + third
    return quantity, third, inner - BASIS * third, inner < 3 * BASIS


def split(values):
    high = values.astype(bf16)
    return high, (values - high.astype(f32)).astype(bf16)


def mul(a, b):
    return jnp.dot(a, b, preferred_element_type=f32)


def row_of(quantity):
    return GROUP * (quantity // 3) + BASIS * (quantity % 3)


def kernel(n_dom, n_sub, *refs):
    inputs, out_ref, scratch = refs[:13], refs[13], refs[14:]
    held, scratch = scratch[:13], scratch[13:]
    (
        state_ref,
        geometry_ref,
        scale_ref,
        material_ref,
        cluster_ref,
        neighbours_ref,
        orientation_ref,
        stiffness_ref,
        jacobians_ref,
        local_ref,
        neigh_ref,
        plus_ref,
        minus_ref,
    ) = held
    (
        dofs,
        small,
        basis,
        fluxes,
        wide,
        right,
        hot,
        table,
        own,
        picked_high,
        picked_low,
        ends,
        packed,
        from_sub,
        from_dom,
        load_sem,
        send_sem,
        recv_sem,
    ) = scratch
    count = state_ref.shape[2]
    dom, sub = lax.axis_index("dom"), lax.axis_index("sub")
    left_dev = (lax.rem(dom + n_dom - 1, n_dom), sub)
    right_dev = (lax.rem(dom + 1, n_dom), sub)
    peers = [(dom, lax.rem(sub + k, n_sub)) for k in range(1, n_sub)]

    barrier = pltpu.get_barrier_semaphore()
    for other in [left_dev, right_dev] + peers:
        pl.semaphore_signal(barrier, inc=1, device_id=other, device_id_type=MESH)
    loads = [pltpu.make_async_copy(inputs[i], held[i], load_sem.at[i]) for i in range(13)]
    for i in (7, 8, 0, 1, 3, 4, 2, 5, 6, 9, 10, 11, 12):
        loads[i].start()

    small[...] = jnp.zeros_like(small)
    fluxes[...] = jnp.zeros_like(fluxes)
    right[...] = jnp.zeros_like(right)
    dofs[...] = jnp.zeros_like(dofs)
    col = iota((16, ROWS), 1)
    _, _, fn, ok = place(col)
    hit = (iota((16, ROWS), 0) == fn) & ok
    pick_high = jnp.where(hit & (col < 2 * GROUP), 1.0, 0.0).astype(bf16)
    pick_low = jnp.where(hit & (col >= 2 * GROUP), 1.0, 0.0).astype(bf16)
    _, third_row, fn_row, ok_row = place(iota((GROUP, ROWS), 0))
    _, third_col, _, ok_col = place(iota((GROUP, ROWS), 1) & (GROUP - 1))
    same_third = (third_row == third_col) & ok_row & ok_col
    _, _, fn, ok = place(iota((GROUP, SLOTS * BASIS), 0))
    offset = jnp.where(ok, iota((GROUP, SLOTS * BASIS), 1) - SLOTS * fn, -1)

    def expand(spread, first, last):
        chosen = [jnp.where(offset == k, 1.0, 0.0).astype(bf16) for k in range(first, last)]
        full = mul(jnp.concatenate(chosen, axis=0), spread)
        for k in range(first, last):
            block = full[GROUP * (k - first) : GROUP * (k - first) + GROUP]
            basis[GROUP * k : GROUP * k + GROUP, :] = jnp.where(same_third, block, 0.0).astype(bf16)

    col = iota((16, 128), 1)
    quantity, _, _, ok = place(col)
    pick = jnp.where((quantity == iota((16, 128), 0)) & ok & (col < ROWS), 1.0, 0.0).astype(bf16)
    _, _, fn_row, ok_row = place(iota((ROWS, 128), 0))
    _, _, fn_col, ok_col = place(iota((ROWS, 128), 1))
    same_fn = (fn_row == fn_col) & ok_row & ok_col & (iota((ROWS, 128), 1) < ROWS)
    quantity, _, _, ok = place(iota((ROWS, 16 * QUANT), 0))
    flux_offset = jnp.where(ok, iota((ROWS, 16 * QUANT), 1) - 16 * quantity, -1)

    def expand_fluxes(slots, blocks):
        high, low = split(fluxes[...].reshape(16 * QUANT, 128)[:, :16])
        spread_high, spread_low = mul(high, pick).astype(bf16), mul(low, pick).astype(bf16)
        spread = jnp.concatenate([spread_high, spread_low], axis=1)
        for m in range(3):
            chosen = [jnp.where(flux_offset == slot[m], 1.0, 0.0).astype(bf16) for slot in slots]
            full = mul(jnp.concatenate(chosen, axis=0), spread)
            for i, (one, two, three) in enumerate(blocks):
                part = full[ROWS * i : ROWS * i + ROWS]
                high = jnp.where(same_fn, part[:, :128], 0.0).astype(bf16)
                low = jnp.where(same_fn, part[:, 128:], 0.0).astype(bf16)
                rows = slice(ROWS * m, ROWS * m + ROWS)
                wide[rows, 128 * one : 128 * one + 128] = high
                wide[rows, 128 * two : 128 * two + 128] = high
                wide[rows, 128 * three : 128 * three + 128] = low

    loads[7].wait()
    small[:, :3, :BASIS] = stiffness_ref[...]
    high, low = split(small[...].reshape(SLOTS * BASIS, 128)[:, :16])
    expand((mul(high, pick_high) + mul(low, pick_low)).astype(bf16), 0, 3)

    loads[8].wait()
    for m in range(3):
        fluxes[:, 3 * m : 3 * m + 3, :QUANT] = jacobians_ref[m]
    expand_fluxes([(c, 3 + c, 6 + c) for c in range(3)], [(c, 3 + c, 6 + c) for c in range(3)])

    loads[0].wait()
    for v in range(QUANT):
        dofs[row_of(v) : row_of(v) + BASIS, :] = state_ref[v]
    for i in (1, 3, 4):
        loads[i].wait()
    material = jnp.broadcast_to(material_ref[...], (ROWS, count))
    coarse = jnp.broadcast_to(cluster_ref[...], (ROWS, count)).astype(f32)

    def on_basis(high, low, first, last):
        parts = []
        for g in range(3):
            h, l = high[GROUP * g : GROUP * g + GROUP], low[GROUP * g : GROUP * g + GROUP]
            parts.append(mul(basis[GROUP * first : GROUP * last, :], jnp.concatenate([h, l, h], axis=0)))
        return [
            jnp.concatenate([part[GROUP * k : GROUP * k + GROUP] for part in parts], axis=0)
            for k in range(last - first)
        ]

    def put(values, blocks, start, length):
        high, low = split(values)
        for block, half in zip(blocks, (high, low, high)):
            right[128 * block + start : 128 * block + start + length, :] = half

    def mixtures(mapped):
        for c in range(3):
            mixture = (
                mapped[0] * geometry_ref[0, c : c + 1, :]
                + mapped[1] * geometry_ref[1, c : c + 1, :]
                + mapped[2] * geometry_ref[2, c : c + 1, :]
            )
            put(mixture, (c, 3 + c, 6 + c), 0, ROWS)

    def on_quantities(first, last):
        every = mul(wide[:, 128 * first : 128 * last], right[128 * first : 128 * last, :])
        return jnp.where(
            material == 0,
            every[:ROWS],
            jnp.where(material == 1, every[ROWS : 2 * ROWS], every[2 * ROWS :]),
        )

    def star(values):
        high, low = split(values)
        mixtures(on_basis(high, low, 0, 3))
        return on_quantities(0, 9)

    def predict(values, shifted):
        first = -star(values)
        second = -star(first)
        if shifted:
            values = values + coarse * (step_length * first + 0.5 * step_length**2 * second)
            first = first + coarse * (step_length * second)
        return step_length * values + step_length**2 / 2 * first + step_length**3 / 6 * second

    def halves(values, lanes):
        high, low = split(values)
        table[:ROWS, lanes] = high
        table[ROWS:, lanes] = low

    lane = iota((ROWS // 2, COPY_DEV), 1)
    front = lane < SUB_COPY

    def send(integral, r):
        ends[r, 0] = integral[:, :COPY_DEV]
        ends[r, 1] = integral[:, count - COPY_DEV :]
        top, bottom = integral[: ROWS // 2, :COPY_DEV], integral[ROWS // 2 :, :COPY_DEV]
        mine = jnp.where(front, top, pltpu.roll(bottom, SUB_COPY, 1))
        packed[r] = mine
        from_sub[r, sub] = mine
        if r == 0:
            pl.semaphore_wait(barrier, n_sub + 1)
        copies = []
        for k, (end, other) in enumerate([(1, right_dev), (0, left_dev)]):
            copies.append(
                pltpu.make_async_remote_copy(
                    src_ref=ends.at[r, end],
                    dst_ref=from_dom.at[r, k],
                    send_sem=send_sem.at[r, k],
                    recv_sem=recv_sem.at[r, k],
                    device_id=other,
                    device_id_type=MESH,
                )
            )
        for k, other in enumerate(peers):
            copies.append(
                pltpu.make_async_remote_copy(
                    src_ref=packed.at[r],
                    dst_ref=from_sub.at[r, sub],
                    send_sem=send_sem.at[r, 2 + k],
                    recv_sem=recv_sem.at[r, 2 + k],
                    device_id=other,
                    device_id_type=MESH,
                )
            )
        for copy in copies:
            copy.start()
        return copies

    depth = hot.shape[0]

    def prepare():
        for i in (2, 5, 6, 9, 10, 11, 12):
            loads[i].wait()
        for f in range(4):
            wanted = jnp.broadcast_to(neighbours_ref[f : f + 1, :], (depth, count))
            hit = jnp.where(iota((depth, count), 0) == wanted, 1.0, 0.0)
            hot[:, count * f : count * f + count] = hit.astype(bf16)
        small[:, 6:10, :BASIS] = local_ref[...]
        small[:, 10:22, :BASIS] = neigh_ref[...]
        high, low = split(small[...].reshape(SLOTS * BASIS, 128)[:, :16])
        expand((mul(high, pick_high) + mul(low, pick_low)).astype(bf16), 6, 22)
        which = iota((16, SLOTS * BASIS), 1) - SLOTS * iota((16, SLOTS * BASIS), 0)
        _, _, fn, ok = place(iota((GROUP, 16), 0))
        repeat = jnp.where((fn == iota((GROUP, 16), 1)) & ok, 1.0, 0.0).astype(bf16)
        for k in range(3):
            chosen = jnp.where(which == k, 1.0, 0.0).astype(bf16)
            h, l = mul(chosen, high).T.astype(bf16), mul(chosen, low).T.astype(bf16)
            block = mul(repeat, (mul(h, pick_high) + mul(l, pick_low)).astype(bf16))
            rows = slice(GROUP * (3 + k), GROUP * (4 + k))
            basis[rows, :] = jnp.where(same_third, block, 0.0).astype(bf16)
        fluxes[:, 9:12, :QUANT] = -plus_ref[...]
        fluxes[:, 12:15, :QUANT] = -minus_ref[...]
        expand_fluxes([(9, 10, 11), (12, 13, 14)], [(9, 10, 11), (12, 13, 14)])

    def advance(values, r):
        integral = predict(values, r == 1)
        copies = send(integral, r)
        if r == 0:
            prepare()
        high, low = split(integral)
        table[:ROWS, :count] = high
        table[ROWS:, :count] = low
        mapped = on_basis(high, low, 3, 10)
        mixtures(mapped[:3])
        local = mapped[3] * scale_ref[0:1, :]
        for f in range(1, 4):
            local = local + mapped[3 + f] * scale_ref[f : f + 1, :]
        put(local, (9, 10, 11), 0, ROWS)
        change = on_quantities(0, 12)
        for f in range(4):
            lanes = slice(count * f, count * f + count)
            own[:, lanes] = mul(table[:, :count], hot[:count, lanes]).astype(bf16)

        for copy in copies:
            copy.wait()
        for pair in range(n_sub // 2):
            one, two = from_sub[r, 2 * pair], from_sub[r, 2 * pair + 1]
            top = jnp.where(front, one, pltpu.roll(two, SUB_COPY, 1))
            bottom = jnp.where(front, pltpu.roll(one, SUB_COPY, 1), two)
            lanes = slice(count + 128 * pair, count + 128 * pair + 128)
            halves(jnp.concatenate([top, bottom], axis=0), lanes)
        for k in range(2):
            start = count + SUB_COPY * n_sub + COPY_DEV * k
            halves(from_dom[r, k], slice(start, start + COPY_DEV))

        totals = [0.0] * 3
        for f in range(4):
            lanes = slice(count * f, count * f + count)
            found = mul(table[:, count:], hot[count:, lanes]).astype(bf16) + own[:, lanes]
            picked_high[:, lanes] = found[:ROWS]
            picked_low[:, lanes] = found[ROWS:]
            for g in range(3):
                rows = slice(GROUP * g, GROUP * g + GROUP)
                h, l = picked_high[rows, lanes], picked_low[rows, lanes]
                turned = mul(basis[10 * GROUP :, :], jnp.concatenate([h, l, h], axis=0))
                turn = jnp.broadcast_to(orientation_ref[f : f + 1, :], (GROUP, count))
                chosen = turned[:GROUP]
                for t in range(1, 12):
                    chosen = jnp.where(turn == t, turned[GROUP * t : GROUP * t + GROUP], chosen)
                totals[g] = totals[g] + chosen * scale_ref[f : f + 1, :]
        for g in range(3):
            put(totals[g], (12, 13, 14), GROUP * g, GROUP)
        return change + on_quantities(12, 15)

    state = dofs[...]
    first_change = advance(state, 0)
    middle = state + (1.0 - coarse) * first_change
    second_change = advance(middle, 1)
    dofs[...] = middle + second_change + coarse * first_change
    for v in range(QUANT):
        out_ref[v] = dofs[row_of(v) : row_of(v) + BASIS, :]


def shards(n_dom, n_sub, state, geometry, face_scale, material, cluster, neighbours, orientation, *parameters):
    stiffness, jacobians, flux_local, flux_neigh, flux_plus, flux_minus = parameters
    count = state.shape[2]
    depth = count + SUB_COPY * n_sub + 2 * COPY_DEV
    operands = [
        state,
        geometry,
        face_scale,
        material[None],
        cluster[None],
        neighbours,
        orientation,
        stiffness.transpose(1, 0, 2),
        jacobians.transpose(0, 2, 1, 3),
        flux_local.transpose(1, 0, 2),
        flux_neigh.transpose(1, 0, 2),
        flux_plus.transpose(1, 0, 2),
        flux_minus.transpose(1, 0, 2),
    ]
    copies = n_sub + 1
    return pl.pallas_call(
        functools.partial(kernel, n_dom, n_sub),
        out_shape=jax.ShapeDtypeStruct(state.shape, f32),
        in_specs=[pl.BlockSpec(memory_space=pltpu.HBM)] * 13,
        out_specs=pl.BlockSpec(memory_space=pltpu.VMEM),
        scratch_shapes=[pltpu.VMEM(x.shape, x.dtype) for x in operands]
        + [
            pltpu.VMEM((ROWS, count), f32),
            pltpu.VMEM((BASIS, SLOTS, 128), f32),
            pltpu.VMEM((22 * GROUP, ROWS), bf16),
            pltpu.VMEM((QUANT, 16, 128), f32),
            pltpu.VMEM((3 * ROWS, 15 * 128), bf16),
            pltpu.VMEM((15 * 128, count), bf16),
            pltpu.VMEM((depth, 4 * count), bf16),
            pltpu.VMEM((2 * ROWS, depth), bf16),
            pltpu.VMEM((2 * ROWS, 4 * count), bf16),
            pltpu.VMEM((ROWS, 4 * count), bf16),
            pltpu.VMEM((ROWS, 4 * count), bf16),
            pltpu.VMEM((2, 2, ROWS, COPY_DEV), f32),
            pltpu.VMEM((2, ROWS // 2, COPY_DEV), f32),
            pltpu.VMEM((2, n_sub, ROWS // 2, COPY_DEV), f32),
            pltpu.VMEM((2, 2, ROWS, COPY_DEV), f32),
            pltpu.SemaphoreType.DMA((13,)),
            pltpu.SemaphoreType.DMA((2, copies)),
            pltpu.SemaphoreType.DMA((2, copies)),
        ],
        compiler_params=pltpu.CompilerParams(
            collective_id=0, has_side_effects=True, vmem_limit_bytes=LIMIT
        ),
    )(*operands)


def solution(mesh):
    placed = (
        P(None, None, ("dom", "sub")),
        P(None, None, ("dom", "sub")),
        P(None, ("dom", "sub")),
        P(("dom", "sub")),
        P(("dom", "sub")),
        P(None, ("dom", "sub")),
        P(None, ("dom", "sub")),
        P(),
        P(),
        P(),
        P(),
        P(),
        P(),
    )
    return jax.shard_map(
        functools.partial(shards, mesh.shape["dom"], mesh.shape["sub"]),
        mesh=mesh,
        in_specs=placed,
        out_specs=P(None, None, ("dom", "sub")),
        check_vma=False,
    )
```

time: 22.6 us -> 22 us (0.973)
  local copies, waits for them, and re-layouts: 3.82 us -> 1.58 us
  Pallas kernels: 18.4 us -> 20.2 us
    unnamed x31 -> x1, local copies, waits for them, and re-layouts: 3.82 us -> 1.58 us
    pallas_call x1, Pallas kernels: 18.4 us -> 20.2 us  [shards(): pl.pallas_call(functools.partial(kernel, n_dom, n_sub), out_shape=jax.Sha...]
where the time goes in v2:
time: 22 us; the launch traced here: 21.8 us
  Pallas kernels  20.2 us (92%)
  local copies, waits for them, and re-layouts  1.58 us (7%)
    pallas_call x1, Pallas kernels, shards(): pl.pallas_call(functools.partial(kernel, n_dom, n_sub), out_shape=jax.Sha...  20.2 us
    unnamed x1, local copies, waits for them, and re-layouts  1.58 us

profile of v2, /device:TPU:0, one launch (start us, length us, event | category | flops | bytes accessed | tf_op | source)
XLA Modules:
  0.0 21.8 jit_solution(3125205443064092292)
XLA Ops:
  0.0 20.2 %shard_map.127 = f32[9,10,256]{2,1,0:T(8,128)} custom-call(f32[9,10,256]{2,1,0:T(8,128)} %refs_0_.1, f32[3,3,256]{2,1,0:T(4,128)} %refs_1_.1, f32[4,256]{1,0:T(4,128)} %refs_2_.1, s32[1,256]{1,0:T(1,128)} %bitcast.14, s32[1,256]{1,0:T(1,128)} %bitcast.15, s32[4,256]{1,0:T(4,128)} %refs_5_.1, s32[4,256]{1,0:T(4,128)} %refs_6_.1, f32[10,3,10]{2,1,0:T(4,128)} %bitcast.10, ...), custom_call_target="tpu_custom_call" | custom-call | tf_op jit(solution)/shard_map/pallas_call | solution.py:359
  20.3 1.6 %copy.15 = f32[9,10,256]{2,1,0:T(8,128)} copy(f32[9,10,256]{2,1,0:T(8,128)} %shard_map.127) | data formatting | bytes 184320

commit v3 on v2

--- a/solution.py
+++ b/solution.py
@@ -14,7 +14,7 @@
 GROUP = 32
 ROWS = 96
 SLOTS = 24
-LIMIT = 62 * 1024 * 1024
+LIMIT = 56 * 1024 * 1024
 
 step_length = 0.2
 f32 = jnp.float32
@@ -66,6 +66,7 @@
     ) = held
     (
         dofs,
+        extra,
         small,
         basis,
         fluxes,
@@ -101,6 +102,7 @@
     fluxes[...] = jnp.zeros_like(fluxes)
     right[...] = jnp.zeros_like(right)
     dofs[...] = jnp.zeros_like(dofs)
+    extra[...] = jnp.zeros_like(extra)
     col = iota((16, ROWS), 1)
     _, _, fn, ok = place(col)
     hit = (iota((16, ROWS), 0) == fn) & ok
@@ -144,21 +146,18 @@
                 wide[rows, 128 * two : 128 * two + 128] = high
                 wide[rows, 128 * three : 128 * three + 128] = low
 
-    loads[7].wait()
+    for i in (7, 8, 0, 1, 3, 4):
+        loads[i].wait()
     small[:, :3, :BASIS] = stiffness_ref[...]
     high, low = split(small[...].reshape(SLOTS * BASIS, 128)[:, :16])
     expand((mul(high, pick_high) + mul(low, pick_low)).astype(bf16), 0, 3)
 
-    loads[8].wait()
     for m in range(3):
         fluxes[:, 3 * m : 3 * m + 3, :QUANT] = jacobians_ref[m]
     expand_fluxes([(c, 3 + c, 6 + c) for c in range(3)], [(c, 3 + c, 6 + c) for c in range(3)])
 
-    loads[0].wait()
     for v in range(QUANT):
         dofs[row_of(v) : row_of(v) + BASIS, :] = state_ref[v]
-    for i in (1, 3, 4):
-        loads[i].wait()
     material = jnp.broadcast_to(material_ref[...], (ROWS, count))
     coarse = jnp.broadcast_to(cluster_ref[...], (ROWS, count)).astype(f32)
 
@@ -202,9 +201,8 @@
     def predict(values, shifted):
         first = -star(values)
         second = -star(first)
-        if shifted:
-            values = values + coarse * (step_length * first + 0.5 * step_length**2 * second)
-            first = first + coarse * (step_length * second)
+        values = values + shifted * (step_length * first + 0.5 * step_length**2 * second)
+        first = first + shifted * (step_length * second)
         return step_length * values + step_length**2 / 2 * first + step_length**3 / 6 * second
 
     def halves(values, lanes):
@@ -222,8 +220,6 @@
         mine = jnp.where(front, top, pltpu.roll(bottom, SUB_COPY, 1))
         packed[r] = mine
         from_sub[r, sub] = mine
-        if r == 0:
-            pl.semaphore_wait(barrier, n_sub + 1)
         copies = []
         for k, (end, other) in enumerate([(1, right_dev), (0, left_dev)]):
             copies.append(
@@ -278,10 +274,10 @@
         expand_fluxes([(9, 10, 11), (12, 13, 14)], [(9, 10, 11), (12, 13, 14)])
 
     def advance(values, r):
-        integral = predict(values, r == 1)
+        integral = predict(values, coarse * r.astype(f32))
+        pl.when(r == 0)(lambda: pl.semaphore_wait(barrier, n_sub + 1))
         copies = send(integral, r)
-        if r == 0:
-            prepare()
+        pl.when(r == 0)(prepare)
         high, low = split(integral)
         table[:ROWS, :count] = high
         table[ROWS:, :count] = low
@@ -327,11 +323,14 @@
             put(totals[g], (12, 13, 14), GROUP * g, GROUP)
         return change + on_quantities(12, 15)
 
-    state = dofs[...]
-    first_change = advance(state, 0)
-    middle = state + (1.0 - coarse) * first_change
-    second_change = advance(middle, 1)
-    dofs[...] = middle + second_change + coarse * first_change
+    def half_step(r, carry):
+        change = advance(dofs[...], r)
+        later = coarse * change
+        dofs[...] = dofs[...] + extra[...] + (change - (1 - r).astype(f32) * later)
+        extra[...] = later
+        return carry
+
+    lax.fori_loop(0, 2, half_step, 0)
     for v in range(QUANT):
         out_ref[v] = dofs[row_of(v) : row_of(v) + BASIS, :]
 
@@ -358,11 +357,12 @@
     copies = n_sub + 1
     return pl.pallas_call(
         functools.partial(kernel, n_dom, n_sub),
-        out_shape=jax.ShapeDtypeStruct(state.shape, f32),
+        out_shape=pltpu.VMEM(state.shape, f32),
         in_specs=[pl.BlockSpec(memory_space=pltpu.HBM)] * 13,
         out_specs=pl.BlockSpec(memory_space=pltpu.VMEM),
         scratch_shapes=[pltpu.VMEM(x.shape, x.dtype) for x in operands]
         + [
+            pltpu.VMEM((ROWS, count), f32),
             pltpu.VMEM((ROWS, count), f32),
             pltpu.VMEM((BASIS, SLOTS, 128), f32),
             pltpu.VMEM((22 * GROUP, ROWS), bf16),

time: 22 us -> 20.3 us (0.923)
  local copies, waits for them, and re-layouts: 1.58 us -> 0.66 us
  Pallas kernels: 20.2 us -> 19.4 us
    unnamed x1, local copies, waits for them, and re-layouts: 1.58 us -> 0.66 us
    pallas_call x1, Pallas kernels: 20.2 us -> 19.4 us  [shards(): pl.pallas_call(functools.partial(kernel, n_dom, n_sub), out_shape=pltpu.V...]
where the time goes in v3:
time: 20.3 us; the launch traced here: 20.1 us
  Pallas kernels  19.4 us (96%)
  local copies, waits for them, and re-layouts  0.66 us (3%)
    pallas_call x1, Pallas kernels, shards(): pl.pallas_call(functools.partial(kernel, n_dom, n_sub), out_shape=pltpu.V...  19.4 us
    unnamed x1, local copies, waits for them, and re-layouts  0.66 us

profile of v3, /device:TPU:0, one launch (start us, length us, event | category | flops | bytes accessed | tf_op | source)
XLA Modules:
  0.0 20.1 jit_solution(4767072260777826820)
XLA Ops:
  0.0 19.4 %shard_map.127 = f32[9,10,256]{2,1,0:T(8,128)S(1)} custom-call(f32[9,10,256]{2,1,0:T(8,128)} %refs_0_.1, f32[3,3,256]{2,1,0:T(4,128)} %refs_1_.1, f32[4,256]{1,0:T(4,128)} %refs_2_.1, s32[1,256]{1,0:T(1,128)} %bitcast.14, s32[1,256]{1,0:T(1,128)} %bitcast.15, s32[4,256]{1,0:T(4,128)} %refs_5_.1, s32[4,256]{1,0:T(4,128)} %refs_6_.1, f32[10,3,10]{2,1,0:T(4,128)} %bitcast.10, ...), custom_call_target="tpu_custom_call" | custom-call | tf_op jit(solution)/shard_map/pallas_call | solution.py:358
  19.5 0.7 %copy.15 = f32[9,10,256]{2,1,0:T(8,128)} copy(f32[9,10,256]{2,1,0:T(8,128)S(1)} %shard_map.127) | data formatting | bytes 184320

commit v4 on v3

--- a/solution.py
+++ b/solution.py
@@ -252,10 +252,14 @@
     def prepare():
         for i in (2, 5, 6, 9, 10, 11, 12):
             loads[i].wait()
+        number = iota((128, count), 0).astype(f32).astype(bf16)
+        one, zero = jnp.ones((128, count), bf16), jnp.zeros((128, count), bf16)
         for f in range(4):
-            wanted = jnp.broadcast_to(neighbours_ref[f : f + 1, :], (depth, count))
-            hit = jnp.where(iota((depth, count), 0) == wanted, 1.0, 0.0)
-            hot[:, count * f : count * f + count] = hit.astype(bf16)
+            wanted = jnp.broadcast_to(neighbours_ref[f : f + 1, :], (16, count))
+            for start in range(0, depth, 128):
+                near = jnp.clip(wanted - start, -1, 128).astype(f32).astype(bf16)
+                hit = jnp.where(number == jnp.concatenate([near] * 8, axis=0), one, zero)
+                hot[start : start + 128, count * f : count * f + count] = hit
         small[:, 6:10, :BASIS] = local_ref[...]
         small[:, 10:22, :BASIS] = neigh_ref[...]
         high, low = split(small[...].reshape(SLOTS * BASIS, 128)[:, :16])
@@ -288,26 +292,29 @@
             local = local + mapped[3 + f] * scale_ref[f : f + 1, :]
         put(local, (9, 10, 11), 0, ROWS)
         change = on_quantities(0, 12)
-        for f in range(4):
-            lanes = slice(count * f, count * f + count)
-            own[:, lanes] = mul(table[:, :count], hot[:count, lanes]).astype(bf16)
-
-        for copy in copies:
+
+        for copy in copies[2:]:
             copy.wait()
+        near = count + SUB_COPY * n_sub
         for pair in range(n_sub // 2):
             one, two = from_sub[r, 2 * pair], from_sub[r, 2 * pair + 1]
             top = jnp.where(front, one, pltpu.roll(two, SUB_COPY, 1))
             bottom = jnp.where(front, pltpu.roll(one, SUB_COPY, 1), two)
             lanes = slice(count + 128 * pair, count + 128 * pair + 128)
             halves(jnp.concatenate([top, bottom], axis=0), lanes)
+        for f in range(4):
+            lanes = slice(count * f, count * f + count)
+            own[:, lanes] = mul(table[:, :near], hot[:near, lanes]).astype(bf16)
+
+        for copy in copies[:2]:
+            copy.wait()
         for k in range(2):
-            start = count + SUB_COPY * n_sub + COPY_DEV * k
-            halves(from_dom[r, k], slice(start, start + COPY_DEV))
+            halves(from_dom[r, k], slice(near + COPY_DEV * k, near + COPY_DEV * (k + 1)))
 
         totals = [0.0] * 3
         for f in range(4):
             lanes = slice(count * f, count * f + count)
-            found = mul(table[:, count:], hot[count:, lanes]).astype(bf16) + own[:, lanes]
+            found = mul(table[:, near:], hot[near:, lanes]).astype(bf16) + own[:, lanes]
             picked_high[:, lanes] = found[:ROWS]
             picked_low[:, lanes] = found[ROWS:]
             for g in range(3):

time: 20.3 us -> 20.4 us (level)
  no operation moved by 1% of the time
where the time goes in v4:
time: 20.4 us; the launch traced here: 20.3 us
  Pallas kernels  19.6 us (96%)
  local copies, waits for them, and re-layouts  0.66 us (3%)
    pallas_call x1, Pallas kernels, shards(): pl.pallas_call(functools.partial(kernel, n_dom, n_sub), out_shape=pltpu.V...  19.6 us
    unnamed x1, local copies, waits for them, and re-layouts  0.66 us

profile of v4, /device:TPU:0, one launch (start us, length us, event | category | flops | bytes accessed | tf_op | source)
XLA Modules:
  0.0 20.3 jit_solution(11975906117282024589)
XLA Ops:
  0.0 19.6 %shard_map.127 = f32[9,10,256]{2,1,0:T(8,128)S(1)} custom-call(f32[9,10,256]{2,1,0:T(8,128)} %refs_0_.1, f32[3,3,256]{2,1,0:T(4,128)} %refs_1_.1, f32[4,256]{1,0:T(4,128)} %refs_2_.1, s32[1,256]{1,0:T(1,128)} %bitcast.14, s32[1,256]{1,0:T(1,128)} %bitcast.15, s32[4,256]{1,0:T(4,128)} %refs_5_.1, s32[4,256]{1,0:T(4,128)} %refs_6_.1, f32[10,3,10]{2,1,0:T(4,128)} %bitcast.10, ...), custom_call_target="tpu_custom_call" | custom-call | tf_op jit(solution)/shard_map/pallas_call | solution.py:365
  19.6 0.7 %copy.15 = f32[9,10,256]{2,1,0:T(8,128)} copy(f32[9,10,256]{2,1,0:T(8,128)S(1)} %shard_map.127) | data formatting | bytes 184320

commit v5 on v4

--- a/solution.py
+++ b/solution.py
@@ -66,7 +66,6 @@
     ) = held
     (
         dofs,
-        extra,
         small,
         basis,
         fluxes,
@@ -102,7 +101,6 @@
     fluxes[...] = jnp.zeros_like(fluxes)
     right[...] = jnp.zeros_like(right)
     dofs[...] = jnp.zeros_like(dofs)
-    extra[...] = jnp.zeros_like(extra)
     col = iota((16, ROWS), 1)
     _, _, fn, ok = place(col)
     hit = (iota((16, ROWS), 0) == fn) & ok
@@ -201,8 +199,9 @@
     def predict(values, shifted):
         first = -star(values)
         second = -star(first)
-        values = values + shifted * (step_length * first + 0.5 * step_length**2 * second)
-        first = first + shifted * (step_length * second)
+        if shifted:
+            values = values + coarse * (step_length * first + 0.5 * step_length**2 * second)
+            first = first + coarse * (step_length * second)
         return step_length * values + step_length**2 / 2 * first + step_length**3 / 6 * second
 
     def halves(values, lanes):
@@ -278,10 +277,12 @@
         expand_fluxes([(9, 10, 11), (12, 13, 14)], [(9, 10, 11), (12, 13, 14)])
 
     def advance(values, r):
-        integral = predict(values, coarse * r.astype(f32))
-        pl.when(r == 0)(lambda: pl.semaphore_wait(barrier, n_sub + 1))
+        integral = predict(values, r == 1)
+        if r == 0:
+            pl.semaphore_wait(barrier, n_sub + 1)
         copies = send(integral, r)
-        pl.when(r == 0)(prepare)
+        if r == 0:
+            prepare()
         high, low = split(integral)
         table[:ROWS, :count] = high
         table[ROWS:, :count] = low
@@ -330,14 +331,11 @@
             put(totals[g], (12, 13, 14), GROUP * g, GROUP)
         return change + on_quantities(12, 15)
 
-    def half_step(r, carry):
-        change = advance(dofs[...], r)
-        later = coarse * change
-        dofs[...] = dofs[...] + extra[...] + (change - (1 - r).astype(f32) * later)
-        extra[...] = later
-        return carry
-
-    lax.fori_loop(0, 2, half_step, 0)
+    state = dofs[...]
+    first_change = advance(state, 0)
+    middle = state + (1.0 - coarse) * first_change
+    second_change = advance(middle, 1)
+    dofs[...] = middle + second_change + coarse * first_change
     for v in range(QUANT):
         out_ref[v] = dofs[row_of(v) : row_of(v) + BASIS, :]
 
@@ -370,7 +368,6 @@
         scratch_shapes=[pltpu.VMEM(x.shape, x.dtype) for x in operands]
         + [
             pltpu.VMEM((ROWS, count), f32),
-            pltpu.VMEM((ROWS, count), f32),
             pltpu.VMEM((BASIS, SLOTS, 128), f32),
             pltpu.VMEM((22 * GROUP, ROWS), bf16),
             pltpu.VMEM((QUANT, 16, 128), f32),

time: 20.4 us -> 20.2 us (level)
    pallas_call x1, Pallas kernels: 19.6 us -> 19.4 us  [shards(): pl.pallas_call(functools.partial(kernel, n_dom, n_sub), out_shape=pltpu.V...]
where the time goes in v5:
time: 20.2 us; the launch traced here: 20 us
  Pallas kernels  19.4 us (96%)
  local copies, waits for them, and re-layouts  0.66 us (3%)
    pallas_call x1, Pallas kernels, shards(): pl.pallas_call(functools.partial(kernel, n_dom, n_sub), out_shape=pltpu.V...  19.4 us
    unnamed x1, local copies, waits for them, and re-layouts  0.66 us

profile of v5, /device:TPU:0, one launch (start us, length us, event | category | flops | bytes accessed | tf_op | source)
XLA Modules:
  0.0 20.0 jit_solution(1493420387345093309)
XLA Ops:
  0.0 19.4 %shard_map.127 = f32[9,10,256]{2,1,0:T(8,128)S(1)} custom-call(f32[9,10,256]{2,1,0:T(8,128)} %refs_0_.1, f32[3,3,256]{2,1,0:T(4,128)} %refs_1_.1, f32[4,256]{1,0:T(4,128)} %refs_2_.1, s32[1,256]{1,0:T(1,128)} %bitcast.14, s32[1,256]{1,0:T(1,128)} %bitcast.15, s32[4,256]{1,0:T(4,128)} %refs_5_.1, s32[4,256]{1,0:T(4,128)} %refs_6_.1, f32[10,3,10]{2,1,0:T(4,128)} %bitcast.10, ...), custom_call_target="tpu_custom_call" | custom-call | tf_op jit(solution)/shard_map/pallas_call | solution.py:363
  19.4 0.7 %copy.15 = f32[9,10,256]{2,1,0:T(8,128)} copy(f32[9,10,256]{2,1,0:T(8,128)S(1)} %shard_map.127) | data formatting | bytes 184320
